TPU v7x, 256 devices: a whole 4x4x8 slice. The times are simulated.
256 devices in a mesh: dp: 8 (over y, core), expert: 32 (over x, z).
Axes of the slice: x: 4, y: 4, z: 8, core: 2. Of those that a mesh axis runs over, the one named last changes fastest.
Arguments:
- tokens: bfloat16 [2048, 7168], P(('dp', 'expert')), may hold values from -6 to 6
- routes: int32 [2048, 8], P(('dp', 'expert')), may hold values from 0 to 31, all different within a row; in each aligned block of 8 rows (0 to 7, 8 to 15, ...) at most 4 rows name the same one
- group_of: int32 [32], replicated, may hold values from 0 to 7, as said below
- sketch_map: bfloat16 [7168, 64], P('dp'), may hold values from -0.0625 to 0.0625
- gate_weight: bfloat16 [32, 7168, 2048], P('expert', None, 'dp'), may hold values from -0.0625 to 0.0625
- up_weight: bfloat16 [32, 7168, 2048], P('expert', None, 'dp'), may hold values from -0.0625 to 0.0625
- down_weight: bfloat16 [32, 2048, 7168], P('expert', 'dp'), may hold values from -0.125 to 0.125
Outputs:
- cross_moment: float32 [8, 64, 7168], P(None, None, 'dp')
- gram_moment: float32 [8, 64, 64], replicated
- output_sum: float32 [8, 7168], P(None, 'dp')
Inputs may be any that keep to these rules, and one draw needn't show every extreme that they name: `routes`: each row names 8 different experts. Among the 8 rows of one device no expert is named more than 4 times, a bound that some block reaches. `group_of`: every merge group has at least one expert.
All inputs are finite; a program needn't handle non-finite values.
Results may differ from a plain program's by a relative error of at most 0.0065.
Values may be sent and summed in bfloat16 or wider, within the bound.
No kernel may reach another device: no remote copies, remote signals or barrier semaphores. Data moves between devices by JAX's collectives and lax.ppermute only.
A program may use at most 128 MiB of HBM per device.

v0:
```python
import math

import jax
import jax.numpy as jnp
from jax import lax
from jax.sharding import PartitionSpec as P

EXPERTS = 32
GROUPS = 8
CAP = 4


def build_outgoing(route_ids, token_rows, block_count, expert_count, capacity):
    row_total = route_ids.shape[0]
    labels = lax.iota(jnp.int32, expert_count)
    named_hits = jnp.any(route_ids[:, :, None] == labels[None, None, :], axis=1).astype(jnp.int32)
    named_hits = named_hits.reshape(block_count, row_total // block_count, expert_count)
    earlier = jnp.cumsum(named_hits, axis=1) - named_hits
    slot_ids = lax.iota(jnp.int32, capacity)
    chosen = (named_hits[..., None] == 1) & (earlier[..., None] == slot_ids[None, None, None, :])
    chosen = chosen.astype(jnp.bfloat16)
    blocked = token_rows.reshape(block_count, row_total // block_count, token_rows.shape[1])
    placed = jnp.einsum("btec,btd->ebcd", chosen, blocked, preferred_element_type=jnp.float32)
    return placed.astype(jnp.bfloat16).reshape(
        expert_count, block_count * capacity, token_rows.shape[1]
    )


def shards(tokens, routes, group_of, sketch_map, gate_weight, up_weight, down_weight):
    local_count = gate_weight.shape[0]
    gathered = (
        lax.all_gather(tokens, "dp", axis=0, tiled=True),
        lax.all_gather(routes, "dp", axis=0, tiled=True),
    )
    outgoing = build_outgoing(gathered[1], gathered[0], lax.axis_size("dp"), EXPERTS, CAP)
    slot_rows = lax.all_to_all(outgoing, "expert", split_axis=0, concat_axis=1, tiled=True)
    gate_part = jnp.einsum(
        "erd,edf->erf", slot_rows, gate_weight, preferred_element_type=jnp.float32
    )
    up_part = jnp.einsum("erd,edf->erf", slot_rows, up_weight, preferred_element_type=jnp.float32)
    hidden = (jax.nn.silu(gate_part) * up_part).astype(jnp.bfloat16)
    column_width = sketch_map.shape[0]
    offset = lax.axis_index("dp") * column_width
    columns = lax.dynamic_slice_in_dim(slot_rows, offset, column_width, 2)
    partial_value = jnp.einsum(
        "erd,dk->erk", columns, sketch_map, preferred_element_type=jnp.float32
    )
    sketch = lax.psum(partial_value, "dp").astype(jnp.bfloat16)
    inner_part = jnp.einsum("erk,erf->ekf", sketch, hidden, preferred_element_type=jnp.float32)
    hidden_total = jnp.sum(hidden, axis=1, dtype=jnp.float32)
    down_wide = down_weight.astype(jnp.float32)
    cross_part = jnp.einsum("ekf,efd->ekd", inner_part, down_wide, precision=lax.Precision.HIGHEST)
    total_part = jnp.einsum("ef,efd->ed", hidden_total, down_wide, precision=lax.Precision.HIGHEST)
    gram_part = jnp.einsum("erk,erj->ekj", sketch, sketch, preferred_element_type=jnp.float32)
    cross_cols, total_cols = (
        lax.psum_scatter(cross_part, "dp", scatter_dimension=2, tiled=True),
        lax.psum_scatter(total_part, "dp", scatter_dimension=1, tiled=True),
    )
    first_expert = lax.axis_index("expert") * local_count
    own_groups = lax.dynamic_slice_in_dim(group_of, first_expert, local_count, 0)
    member = (own_groups[None, :] == lax.iota(jnp.int32, GROUPS)[:, None]).astype(jnp.float32)
    factor = 1.0 / math.sqrt(slot_rows.shape[1])
    term_cross = (
        jnp.einsum("ge,ekc->gkc", member, cross_cols, precision=lax.Precision.HIGHEST) * factor
    )
    term_gram = jnp.einsum("ge,ekj->gkj", member, gram_part, precision=lax.Precision.HIGHEST) * (
        factor * factor
    )
    term_total = (
        jnp.einsum("ge,ec->gc", member, total_cols, precision=lax.Precision.HIGHEST) * factor
    )
    cross_moment, gram_moment, output_sum = lax.psum((term_cross, term_gram, term_total), "expert")
    return (cross_moment, gram_moment, output_sum)


def solution(mesh):
    placed = (
        P(("dp", "expert"), None),
        P(("dp", "expert"), None),
        P(),
        P("dp", None),
        P("expert", None, "dp"),
        P("expert", None, "dp"),
        P("expert", "dp", None),
    )
    return jax.shard_map(
        shards,
        mesh=mesh,
        in_specs=placed,
        out_specs=(P(None, None, "dp"), P(), P(None, "dp")),
        check_vma=False,
    )
```

profile of v0, /device:TPU:16, one launch (start us, length us, event | category | flops | bytes accessed | tf_op | source)
XLA Modules:
  0.0 705.4 jit_solution(3129515640410465756)
XLA Ops:
  7.2 0.0 copy-start
  7.2 13.1 %all_gather.6 = s32[64,8]{1,0:T(8,128)S(1)} all-gather(s32[8,8]{1,0:T(8,128)} %param.8), channel_id=1, replica_groups=mesh['dp'=8,'expert'=32] {'dp'}, dimensions={0}, use_global_device_ids=true | all-gather | bytes 2304 | tf_op jit(solution)/shard_map/all_gather | solution.py:33
  20.3 0.1 copy.16
  20.4 0.1 copy.17
  20.5 13.8 %all_gather.7 = bf16[64,7168]{1,0:T(8,128)(2,1)S(1)} all-gather(bf16[8,7168]{1,0:T(8,128)(2,1)} %param.7), channel_id=1, replica_groups=mesh['dp'=8,'expert'=32] {'dp'}, dimensions={0}, use_global_device_ids=true | all-gather | bytes 1032192 | tf_op jit(solution)/shard_map/all_gather | solution.py:32
  34.4 4.2 convolution_convert_fusion
  38.6 10.2 %copy.18 = bf16[32,32,7168]{2,1,0:T(8,128)(2,1)} copy(bf16[32,32,7168]{2,0,1:T(8,128)(2,1)S(1)} %bitcast.62) | data formatting | bytes 29360128 | tf_op jit(solution)/shard_map/reshape | solution.py:24
  48.8 10.1 %all-to-all-start = ((bf16[32,32,7168]{2,1,0:T(8,128)(2,1)}), bf16[32,32,7168]{2,1,0:T(8,128)(2,1)}, u32[]{:S(2)}, u32[]{:S(2)}) async-start(bf16[32,32,7168]{2,1,0:T(8,128)(2,1)} %copy.18), calls=%async_computation | async-start | bytes 29360128 | tf_op jit(solution)/shard_map/all_to_all | solution.py:36
  58.9 0.0 reduce-scatter.5.cloned.1.call-start
  59.0 334.8 %all-to-all-done = bf16[32,32,7168]{2,1,0:T(8,128)(2,1)} async-done(((bf16[32,32,7168]{2,1,0:T(8,128)(2,1)}), bf16[32,32,7168]{2,1,0:T(8,128)(2,1)}, u32[]{:S(2)}, u32[]{:S(2)}) %all-to-all-start) | async-done | bytes 14680096 | tf_op jit(solution)/shard_map/all_to_all | solution.py:36
  393.7 0.0 copy-done
  393.7 2.2 fusion.15
  395.9 26.7 %all-reduce.5 = bf16[1,1024,64]{1,2,0:T(8,128)(2,1)S(1)} all-reduce(f32[1,1024,64]{1,2,0:T(8,128)S(1)} %fusion.15), channel_id=1, replica_groups=mesh['dp'=8,'expert'=32] {'dp'}, use_global_device_ids=true, to_apply=%region_2.3 | all-reduce | flops 65536 | bytes 393216 | tf_op jit(solution)/shard_map/psum | solution.py:48
  422.6 0.0 copy-start.4
  422.6 8.5 %fusion.4 = f32[1024,256]{1,0:T(8,128)S(1)} fusion(bf16[1024,7168]{1,0:T(8,128)(2,1)} %bitcast.12, bf16[1,7168,256]{2,1,0:T(8,128)(2,1)} %param.11), kind=kOutput, calls=%fused_computation.7 | convolution fusion | flops 3758096384 | bytes 19398656 | tf_op jit(solution)/shard_map/erd,edf->erf/dot_general | solution.py:37
  431.1 0.0 copy-done.4
  431.1 0.0 copy-start.2
  431.1 7.7 %convert_reduce_fusion = (f32[256]{0:T(256)S(1)}, bf16[1024,256]{1,0:T(8,128)(2,1)S(1)}) fusion(bf16[1024,7168]{1,0:T(8,128)(2,1)} %bitcast.12, bf16[1,7168,256]{2,1,0:T(8,128)(2,1)S(1)} %copy-done.4, f32[1024,256]{1,0:T(8,128)S(1)} %fusion.4), kind=kOutput, calls=%fused_computation.16 | convolution fusion | flops 3760193280 | bytes 19923968 | tf_op jit(solution)/shard_map/erd,edf->erf/dot_general | solution.py:40
  438.8 0.2 fusion.21
  439.0 0.0 copy-done.2
  439.0 0.0 copy-start.5
  439.0 3.2 convolution_bitcast_fusion.1
  442.3 0.0 reduce-scatter.5.cloned.1.call-update
  442.3 0.2 reduce-scatter.7.cloned.1.call-start
  442.5 0.0 copy-done.5
  442.6 0.6 dynamic_slice.6
  443.1 0.6 fusion.30
  443.8 0.7 compare_convert_fusion
  444.5 0.2 fusion.19
  444.6 0.8 multiply_multiply_fusion.1
  445.4 7.8 %convolution_bitcast_fusion = f32[7168,1]{1,0:T(8,128)} fusion(f32[256,1]{0,1:T(1,128)S(1)} %bitcast.65, bf16[1,256,7168]{2,1,0:T(8,128)(2,1)} %param.13), kind=kOutput, calls=%fused_computation.1 | convolution fusion | flops 22020096 | bytes 3699712
  453.2 0.0 reduce-scatter.7.cloned.1.call-update
  453.2 0.0 all-reduce.4.cloned.1.call-start
  453.3 39.0 %reduce-scatter.5.cloned.1.call-done = f32[1,64,896]{2,1,0:T(8,128)} async-done(((f32[1,64,7168]{2,1,0:T(8,128)}), f32[1,64,896]{2,1,0:T(8,128)}) %reduce-scatter.5.cloned.1.call-update) | async-done | bytes 229392 | tf_op jit(solution)/shard_map/reduce_scatter | solution.py:56
  492.3 0.0 copy-start.1
  492.3 2.4 multiply_multiply_fusion
  494.7 0.0 all-reduce.4.cloned.1.call-update
  494.7 38.4 %reduce-scatter.7.cloned.1.call-done = f32[896,1]{1,0:T(8,128)} async-done(((f32[7168,1]{1,0:T(8,128)}), f32[896,1]{1,0:T(8,128)}) %reduce-scatter.7.cloned.1.call-update) | async-done | bytes 3600
  533.2 1.2 bitcast_reduce_fusion
  534.4 0.1 multiply_multiply_fusion.2
  534.5 143.2 %psum.31 = f32[8,896]{1,0:T(8,128)} all-reduce(f32[8,896]{1,0:T(8,128)S(1)} %multiply_multiply_fusion.2), channel_id=1, replica_groups=mesh['dp'=8,'expert'=32] {'expert'}, use_global_device_ids=true, to_apply=%region_8.9 | all-reduce | flops 7168 | bytes 57344 | tf_op jit(solution)/shard_map/psum | solution.py:72
  677.7 17.6 %all-reduce.4.cloned.1.call-done = (f32[8,64,896]{2,1,0:T(8,128)}, f32[8,64,64]{2,1,0:T(8,128)}) async-done(((f32[8,64,896]{2,1,0:T(8,128)}, f32[8,64,64]{2,1,0:T(8,128)}), (f32[8,64,896]{2,1,0:T(8,128)}, f32[8,64,64]{2,1,0:T(8,128)})) %all-reduce.4.cloned.1.call-update) | async-done | bytes 1966096 | tf_op jit(solution)/shard_map/psum | solution.py:72
  695.3 0.0 copy-start.3
  695.3 2.9 copy.26
  698.2 0.0 copy-done.3
  698.2 0.7 copy.27
  698.9 0.0 copy-done.1
  (5 shorter events, 0.1 us)
Async XLA Ops:
  7.2 386.6 %copy-start = (bf16[896,64]{0,1:T(8,128)(2,1)S(1)}, bf16[896,64]{0,1:T(8,128)(2,1)}, u32[]{:S(2)}) copy-start(bf16[896,64]{0,1:T(8,128)(2,1)} %param.10) | copy-start | bytes 344068
  48.8 345.0 %all-to-all-start = ((bf16[32,32,7168]{2,1,0:T(8,128)(2,1)}), bf16[32,32,7168]{2,1,0:T(8,128)(2,1)}, u32[]{:S(2)}, u32[]{:S(2)}) async-start(bf16[32,32,7168]{2,1,0:T(8,128)(2,1)} %copy.18), calls=%async_computation | async-start | bytes 29360128 | tf_op jit(solution)/shard_map/all_to_all | solution.py:36
  58.9 433.4 %reduce-scatter.5.cloned.1.call-start = ((), (), s32[]{:S(2)}) async-start(), calls=%async_computation.3 | async-start | bytes 2064384 | tf_op jit(solution)/shard_map/reduce_scatter | solution.py:56
  422.6 8.5 %copy-start.4 = (bf16[1,7168,256]{2,1,0:T(8,128)(2,1)S(1)}, bf16[1,7168,256]{2,1,0:T(8,128)(2,1)}, u32[]{:S(2)}) copy-start(bf16[1,7168,256]{2,1,0:T(8,128)(2,1)} %param.12) | copy-start | bytes 11010052
  431.1 8.0 %copy-start.2 = (bf16[1,256,7168]{2,1,0:T(8,128)(2,1)S(1)}, bf16[1,256,7168]{2,1,0:T(8,128)(2,1)}, u32[]{:S(2)}) copy-start(bf16[1,256,7168]{2,1,0:T(8,128)(2,1)} %param.13) | copy-start | bytes 11010052
  439.0 3.5 copy-start.5
  442.3 90.9 %reduce-scatter.7.cloned.1.call-start = ((), (), s32[]{:S(2)}) async-start(), calls=%async_computation.4 | async-start | bytes 4128768
  453.2 242.1 %all-reduce.4.cloned.1.call-start = ((), (), s32[]{:S(2)}) async-start(), calls=%async_computation.5 | async-start | bytes 4194304 | tf_op jit(solution)/shard_map/psum | solution.py:72
  492.3 206.6 %copy-start.1 = (bf16[896,64]{0,1:T(8,128)(2,1)S(1)}, bf16[896,64]{0,1:T(8,128)(2,1)}, u32[]{:S(2)}) copy-start(bf16[896,64]{0,1:T(8,128)(2,1)} %param.10) | copy-start | bytes 344068
  695.3 2.9 copy-start.3
Sparse Core Ops, SparseCore 0:
  442.4 49.8 reduce-scatter.4
  494.8 38.2 reduce-scatter.6
  537.4 157.8 all-reduce.3
where the time goes:
time: 706 us; the launch traced here: 705 us
  waiting for transfers between devices  430 us (61%)
  blocking collectives  197 us (28%)
  matrix products  33.9 us (5%)
  local copies, waits for them, and re-layouts  15.8 us (2%)
  between operations  13.9 us (2%)
  starting transfers between devices  10.4 us (1%)
    all_to_all x1, waiting for transfers between devices, shards(): lax.all_to_all(outgoing, 'expert', split_axis=0, concat_axis=1, tiled=True)  335 us
    psum x1, blocking collectives, shards(): lax.psum((term_cross, term_gram, term_total), 'expert')  143 us
    reduce_scatter x1, waiting for transfers between devices, shards(): lax.psum_scatter(cross_part, 'dp', scatter_dimension=2, tiled=True)  39 us
    unnamed x4, waiting for transfers between devices  38.5 us
    psum x1, blocking collectives, shards(): sketch = lax.psum(partial_value, 'dp').astype(jnp.bfloat16)  26.7 us
    psum x1, waiting for transfers between devices, shards(): lax.psum((term_cross, term_gram, term_total), 'expert')  17.6 us
  transfers between devices with their start and end apart: 4, of which 4 were waited for; matrix products, arithmetic and copies ran while one was open for 2% of the time, Pallas kernels for 0%

commit v1 on v0

v1 whole, which is shorter than its diff:
```python
import functools
import math

import jax
import jax.numpy as jnp
from jax import lax
from jax.experimental import pallas as pl
from jax.experimental.pallas import tpu as pltpu
from jax.sharding import Mesh
from jax.sharding import PartitionSpec as P

EXPERTS = 32
GROUPS = 8
SKETCH = 64
LANES = 128
ROWS_OUT = 72


def moments_kernel(steps, expert_ref, x_ref, g0_ref, g1_ref, u0_ref, u1_ref, m_ref, tag_ref, out_ref, acc_g, acc_u, acc_s):
    step = pl.program_id(0)
    x = x_ref[...]
    gate = [jnp.dot(x, r[...], preferred_element_type=jnp.float32) for r in (g0_ref, g1_ref)]
    up = [jnp.dot(x, r[...], preferred_element_type=jnp.float32) for r in (u0_ref, u1_ref)]
    part = jnp.dot(x, m_ref[...], preferred_element_type=jnp.float32)

    @pl.when(step == 0)
    def _():
        for i in range(2):
            acc_g[i] = gate[i]
            acc_u[i] = up[i]
        acc_s[...] = part

    @pl.when(step > 0)
    def _():
        for i in range(2):
            acc_g[i] += gate[i]
            acc_u[i] += up[i]
        acc_s[...] += part

    @pl.when(step == steps - 1)
    def _():
        tag = tag_ref[...].astype(jnp.float32)
        lane = lax.broadcasted_iota(jnp.int32, tag.shape, 1)
        mask = jnp.sum(jnp.where(lane == expert_ref[0], tag, 0.0), axis=1, keepdims=True)
        sketch = acc_s[...].astype(jnp.bfloat16)
        wide = sketch.astype(jnp.float32)
        zeros = jnp.zeros((wide.shape[0], ROWS_OUT - SKETCH - 1), jnp.float32)
        left = jnp.concatenate([wide * mask, mask, zeros], axis=1).astype(jnp.bfloat16)
        contract = (((0,), (0,)), ((), ()))
        for i in range(2):
            gated = acc_g[i]
            hidden = (gated / (1.0 + jnp.exp(-gated)) * acc_u[i]).astype(jnp.bfloat16)
            width = hidden.shape[1]
            out_ref[:ROWS_OUT, i * width : (i + 1) * width] = lax.dot_general(
                left, hidden, contract, preferred_element_type=jnp.float32
            )
        for g in range(GROUPS):
            count = jnp.sum(jnp.where(lane == EXPERTS + g, tag, 0.0), axis=1, keepdims=True)
            scaled = wide * count
            high = scaled.astype(jnp.bfloat16)
            low = (scaled - high.astype(jnp.float32)).astype(jnp.bfloat16)
            both = lax.dot_general(sketch, high, contract, preferred_element_type=jnp.float32)
            both += lax.dot_general(sketch, low, contract, preferred_element_type=jnp.float32)
            out_ref[ROWS_OUT:, g * SKETCH : (g + 1) * SKETCH] = both


def local_moments(expert, ext, gates, ups, sketch_map):
    rows = ext.shape[0]
    width, ff = sketch_map.shape[0], gates[0].shape[1]
    depth = 1024
    steps = width // depth
    weight = pl.BlockSpec((depth, ff), lambda k, e: (k, 0))
    return pl.pallas_call(
        functools.partial(moments_kernel, steps),
        grid_spec=pltpu.PrefetchScalarGridSpec(
            num_scalar_prefetch=1,
            grid=(steps,),
            in_specs=[
                pl.BlockSpec((rows, depth), lambda k, e: (0, k)),
                weight,
                weight,
                weight,
                weight,
                pl.BlockSpec((depth, SKETCH), lambda k, e: (k, 0)),
                pl.BlockSpec((rows, LANES), lambda k, e: (0, width // LANES)),
            ],
            out_specs=pl.BlockSpec((ROWS_OUT + SKETCH, 2 * ff), lambda k, e: (0, 0)),
            scratch_shapes=[
                pltpu.VMEM((2, rows, ff), jnp.float32),
                pltpu.VMEM((2, rows, ff), jnp.float32),
                pltpu.VMEM((rows, SKETCH), jnp.float32),
            ],
        ),
        out_shape=jax.ShapeDtypeStruct((ROWS_OUT + SKETCH, 2 * ff), jnp.float32),
        compiler_params=pltpu.CompilerParams(vmem_limit_bytes=48 * 2**20),
        name="local_moments",
    )(expert, ext, *gates, *ups, sketch_map, ext)


def down_kernel(own_ref, other_ref, w0_ref, w1_ref, out_ref):
    width = w0_ref.shape[0]
    total = None
    for left, weight in (
        (own_ref[:, :width] + other_ref[:, width:], w0_ref),
        (own_ref[:, width:] + other_ref[:, :width], w1_ref),
    ):
        high = left.astype(jnp.bfloat16)
        low = (left - high.astype(jnp.float32)).astype(jnp.bfloat16)
        both = jnp.dot(high, weight[...], preferred_element_type=jnp.float32)
        both += jnp.dot(low, weight[...], preferred_element_type=jnp.float32)
        total = both if total is None else total + both
    for t in range(out_ref.shape[1]):
        out_ref[0, t] = total[:, t * LANES : (t + 1) * LANES].astype(out_ref.dtype)


def down_moments(own, other, own_down, other_down, blocks):
    ff, columns = own_down.shape
    block = columns // blocks
    left = pl.BlockSpec((ROWS_OUT, 2 * ff), lambda j: (0, 0))
    weight = pl.BlockSpec((ff, block), lambda j: (0, j))
    return pl.pallas_call(
        down_kernel,
        grid=(blocks,),
        in_specs=[left, left, weight, weight],
        out_specs=pl.BlockSpec((1, block // LANES, ROWS_OUT, LANES), lambda j: (j, 0, 0, 0)),
        out_shape=jax.ShapeDtypeStruct((blocks, block // LANES, ROWS_OUT, LANES), jnp.bfloat16),
        name="down_moments",
    )(own, other, own_down, other_down)


def shards(tokens, routes, group_of, sketch_map, gate_weight, up_weight, down_weight):
    gate, up, down = gate_weight[0], up_weight[0], down_weight[0]
    swap = functools.partial(lax.ppermute, axis_name="core", perm=[(0, 1), (1, 0)])
    core = lax.axis_index("core")
    n_y, n_xz = lax.axis_size("y"), lax.axis_size("x") * lax.axis_size("z")
    expert = lax.axis_index("x") * lax.axis_size("z") + lax.axis_index("z")

    member = (group_of[:, None] == lax.iota(jnp.int32, GROUPS)[None, :]).astype(jnp.float32)
    named = jnp.any(routes[:, :, None] == lax.iota(jnp.int32, EXPERTS), axis=1).astype(jnp.float32)
    counts = jnp.sum(named[:, :, None] * member[None], axis=1)
    tag = jnp.concatenate([named, counts], axis=1).astype(jnp.bfloat16)
    tag = jnp.pad(tag, ((0, 0), (0, LANES - tag.shape[1])))
    ext = jnp.concatenate([tokens, tag], axis=1)
    ext = lax.all_gather(ext, ("y", "x", "z"), axis=0, tiled=True)
    full_map = lax.all_gather(sketch_map, ("y", "core"), axis=0, tiled=True)
    gates, ups = (gate, swap(gate)), (up, swap(up))
    ff, width = down.shape
    halves = down.reshape(ff, n_y, 2, width // (2 * n_y))
    own_down = lax.dynamic_index_in_dim(halves, core, 2, keepdims=False).reshape(ff, width // 2)
    sent = lax.dynamic_index_in_dim(halves, 1 - core, 2, keepdims=False).reshape(ff, width // 2)
    other_down = swap(sent)

    own = local_moments(expert.reshape(1), ext, gates, ups, full_map)
    other = swap(own)
    rows = n_xz * 4 * 8
    factor = 1.0 / math.sqrt(rows)
    gram = (own[ROWS_OUT:] + other[ROWS_OUT:]) * (factor * factor)
    gram_moment = gram.reshape(SKETCH, GROUPS, SKETCH).transpose(1, 0, 2)

    parts = down_moments(own, other, own_down, other_down, n_y)
    parts = lax.all_to_all(parts, "y", split_axis=0, concat_axis=0, tiled=True)
    block = jnp.sum(parts.astype(jnp.float32), axis=0)
    tiles = block.shape[0]
    block = block.reshape(tiles * ROWS_OUT, LANES)
    share = -(-block.shape[0] // (8 * n_xz)) * 8
    block = jnp.pad(block, ((0, share * n_xz - block.shape[0]), (0, 0)))
    pieces = lax.all_to_all(
        block.reshape(n_xz, share, LANES), ("x", "z"), split_axis=0, concat_axis=0, tiled=True
    )
    summed = jnp.einsum("eg,erl->grl", member, pieces, precision=lax.Precision.HIGHEST) * factor
    summed = summed.astype(jnp.bfloat16)
    spread = jnp.broadcast_to(summed[None], (n_xz, *summed.shape))
    spread = lax.all_to_all(spread, ("x", "z"), split_axis=0, concat_axis=0, tiled=True)
    whole = spread.transpose(1, 0, 2, 3).reshape(GROUPS, n_xz * share, LANES)
    whole = whole[:, : tiles * ROWS_OUT].reshape(GROUPS, tiles, ROWS_OUT, LANES)
    whole = whole.astype(jnp.float32).transpose(0, 2, 1, 3).reshape(GROUPS, ROWS_OUT, tiles * LANES)
    return whole[:, :SKETCH], gram_moment, whole[:, SKETCH]


def solution(mesh):
    fine = Mesh(mesh.devices.reshape(4, 2, 4, 8), ("y", "core", "x", "z"))
    dp, expert = ("y", "core"), ("x", "z")
    placed = (
        P((*dp, *expert), None),
        P((*dp, *expert), None),
        P(),
        P(dp, None),
        P(expert, None, dp),
        P(expert, None, dp),
        P(expert, dp, None),
    )
    return jax.shard_map(
        shards,
        mesh=fine,
        in_specs=placed,
        out_specs=(P(None, None, dp), P(), P(None, dp)),
        check_vma=False,
    )
```

time: 706 us -> 273 us (0.39)
  waiting for transfers between devices: 430 us -> 121 us
  blocking collectives: 197 us -> 46.3 us
  matrix products: 33.9 us -> 0.27 us
  Pallas kernels: 0 us -> 33 us
  local copies, waits for them, and re-layouts: 15.8 us -> 45.4 us
    all_to_all x1, waiting for transfers between devices: 335 us -> 25.9 us  [shards(): lax.all_to_all(spread, ('x', 'z'), split_axis=0, concat_axis=0, tiled=True)]
    psum x2 -> x0, blocking collectives: 170 us -> none  [the longest x1 143 us: shards(): lax.psum((term_cross, term_gram, term_total), 'expert')]
    all_gather x0 -> x1, waiting for transfers between devices: none -> 95.2 us  [shards(): ext = lax.all_gather(ext, ('y', 'x', 'z'), axis=0, tiled=True)]
    reduce_scatter x1 -> x0, waiting for transfers between devices: 39 us -> none  [shards(): lax.psum_scatter(cross_part, 'dp', scatter_dimension=2, tiled=True)]
    unnamed x4 -> x1, waiting for transfers between devices: 38.5 us -> 0.02 us
    pallas_call x0 -> x2, Pallas kernels: none -> 33 us  [the longest x1 28.4 us: local_moments(): pl.pallas_call(functools.partial(moments_kernel, steps), grid_spec=pltpu....]
    all_to_all x0 -> x2, blocking collectives: none -> 30.4 us  [the longest x1 18.2 us: shards(): lax.all_to_all(block.reshape(n_xz, share, LANES), ('x', 'z'), split_axis=...]
    dot_general x7 -> x1, matrix products: 26.2 us -> 0.27 us  [shards(): jnp.einsum('eg,erl->grl', member, pieces, precision=lax.Precision.HIGHEST)]
  transfers between devices with their start and end apart: 4 -> 6, of which waited for: 4 -> 3; matrix products, arithmetic and copies ran while one was open for 2% -> 15% of each run, Pallas kernels for 0% -> 11%
where the time goes in v1:
time: 273 us; the launch traced here: 270 us
  waiting for transfers between devices  121 us (44%)
  blocking collectives  46.3 us (17%)
  local copies, waits for them, and re-layouts  45.4 us (17%)
  Pallas kernels  33 us (12%)
  between operations  14.2 us (5%)
  starting transfers between devices  5.38 us (2%)
  other arithmetic  4.37 us (2%)
    all_gather x1, waiting for transfers between devices, shards(): ext = lax.all_gather(ext, ('y', 'x', 'z'), axis=0, tiled=True)  95.2 us
    pallas_call x1, Pallas kernels, local_moments(): pl.pallas_call(functools.partial(moments_kernel, steps), grid_spec=pltpu....  28.4 us
    dynamic_slice x1, local copies, waits for them, and re-layouts, shards(): lax.dynamic_index_in_dim(halves, 1 - core, 2, keepdims=False)  25.9 us
    all_to_all x1, waiting for transfers between devices, shards(): lax.all_to_all(spread, ('x', 'z'), split_axis=0, concat_axis=0, tiled=True)  25.9 us
    all_to_all x1, blocking collectives, shards(): lax.all_to_all(block.reshape(n_xz, share, LANES), ('x', 'z'), split_axis=...  18.2 us
    all_gather x1, blocking collectives, shards(): full_map = lax.all_gather(sketch_map, ('y', 'core'), axis=0, tiled=True)  15.8 us
    all_to_all x1, blocking collectives, shards(): parts = lax.all_to_all(parts, 'y', split_axis=0, concat_axis=0, tiled=True)  12.2 us
    another operation x1, local copies, waits for them, and re-layouts, shards(): halves = down.reshape(ff, n_y, 2, width // (2 * n_y))  9.18 us
  transfers between devices with their start and end apart: 6, of which 3 were waited for; matrix products, arithmetic and copies ran while one was open for 15% of the time, Pallas kernels for 11%

profile of v1, /device:TPU:16, one launch (start us, length us, event | category | flops | bytes accessed | tf_op | source)
XLA Modules:
  0.0 269.9 jit_solution(1926843497271131890)
XLA Ops:
  7.2 0.0 all-gather.2.cloned.1.call-start
  7.2 0.7 fusion.7
  7.9 0.8 fusion.3
  8.7 0.1 multiply_reduce_fusion
  8.8 0.1 fusion.9
  8.8 1.6 pad_maximum_fusion
  10.4 0.0 all-gather.2.cloned.1.call-update
  10.4 0.1 collective-permute-start
  10.5 0.5 collective-permute-start.1
  11.0 9.2 %reshape_squeeze.3 = bf16[256,4,2,896]{3,2,1,0:T(2,128)(2,1)} reshape(bf16[1,256,7168]{2,1,0:T(8,128)(2,1)} %param.13) | data formatting | bytes 7340032 | tf_op jit(solution)/shard_map/reshape;squeeze | solution.py:148
  20.2 25.9 %dynamic-slice_reduce_fusion = (bf16[256,4,896]{2,1,0:T(4,128)(2,1)S(1)}, bf16[256,4,896]{2,1,0:T(4,128)(2,1)}) fusion(bf16[256,4,2,896]{3,2,1,0:T(2,128)(2,1)} %reshape_squeeze.3, s32[]{:T(128)S(6)} %select_n.8, s32[]{:T(128)S(6)} %select_n.7), kind=kLoop, calls=%fused_computation | loop fusion | bytes 7340040 | tf_op jit(solution)/shard_map/jit(dynamic_index_in_dim)/dynamic_slice | solution.py:150
  46.1 0.0 copy-start.4
  46.1 1.6 copy.55
  47.7 0.1 collective-permute-start.3
  47.8 0.0 copy-done.4
  47.8 0.2 copy.42
  47.9 15.8 %all_gather.7.m_ref = bf16[7168,64]{1,0:T(8,128)(2,1)S(1)} all-gather(bf16[896,64]{1,0:T(8,128)(2,1)S(1)} %copy.42), channel_id=1, replica_groups=mesh['y'=4,'core'=2,'x'=4,'z'=8] {'y','core'}, dimensions={0}, use_global_device_ids=true | all-gather | bytes 1032192 | tf_op jit(solution)/shard_map/all_gather | solution.py:145
  63.8 0.0 collective-permute-done.g1_ref
  63.8 0.0 collective-permute-done.1.u1_ref
  63.8 95.2 %all-gather.2.cloned.1.call-done.x_ref.tag_ref = bf16[1024,7296]{1,0:T(8,128)(2,1)} async-done(((bf16[8,7296]{1,0:T(8,128)(2,1)}), bf16[1024,7296]{1,0:T(8,128)(2,1)}) %all-gather.2.cloned.1.call-update) | async-done | bytes 14942224 | tf_op jit(solution)/shard_map/all_gather | solution.py:144
  158.9 0.0 copy-start
  158.9 2.0 copy-done
  161.0 0.0 copy-start.2
  161.0 28.4 %local_moments.1.own_ref = f32[136,512]{1,0:T(8,128)S(1)} custom-call(s32[1]{0:T(128)} %bitcast.1.expert_ref, bf16[1024,7296]{1,0:T(8,128)(2,1)} %all-gather.2.cloned.1.call-done.x_ref.tag_ref, bf16[7168,256]{1,0:T(8,128)(2,1)S(1)} %bitcast.30, bf16[7168,256]{1,0:T(8,128)(2,1)} %collective-permute-done.g1_ref, bf16[7168,256]{1,0:T(8,128)(2,1)} %bitcast.37, ...), custom_call_target="tpu_custom_call" | custom-call | tf_op jit(solution)/shard_map/local_moments/pallas_call | solution.py:73
  189.3 0.0 copy-start.1
  189.4 0.1 collective-permute-start.2
  189.5 0.0 copy-done.2
  189.5 1.5 copy.54
  190.9 0.0 collective-permute-done.3.w1_ref
  190.9 0.1 collective-permute-done.2.other_ref
  191.0 0.0 copy-start.3
  191.0 0.0 copy-done.1
  191.0 0.7 copy-done.3
  191.7 4.6 %down_moments.1 = bf16[4,7,72,128]{3,2,1,0:T(8,128)(2,1)} custom-call(f32[136,512]{1,0:T(8,128)} %copy-done.1, f32[136,512]{1,0:T(8,128)} %copy-done.3, bf16[256,3584]{1,0:T(8,128)(2,1)} %bitcast.31, bf16[256,3584]{1,0:T(8,128)(2,1)} %collective-permute-done.3.w1_ref), custom_call_target="tpu_custom_call" | custom-call | tf_op jit(solution)/shard_map/down_moments/pallas_call | solution.py:121
  196.3 0.0 copy-start.5
  196.3 12.2 %all_to_all.15 = bf16[4,7,72,128]{3,2,1,0:T(8,128)(2,1)S(1)} all-to-all(bf16[4,7,72,128]{3,2,1,0:T(8,128)(2,1)} %down_moments.1), channel_id=1, replica_groups=mesh['y'=4,'core'=2,'x'=4,'z'=8] {'y'}, dimensions={0} | all-to-all | bytes 1032192 | tf_op jit(solution)/shard_map/all_to_all | solution.py:161
  208.6 0.1 convert_reduce_fusion
  208.7 18.2 %all_to_all.16 = f32[32,16,128]{2,1,0:T(8,128)S(1)} all-to-all(f32[32,16,128]{2,1,0:T(8,128)S(1)} %bitcast.38), channel_id=1, replica_groups=mesh['y'=4,'core'=2,'x'=4,'z'=8] {'x','z'}, dimensions={0} | all-to-all | bytes 524288 | tf_op jit(solution)/shard_map/all_to_all | solution.py:167
  226.9 0.0 copy-done.5
  226.9 0.3 fusion
  227.2 1.2 broadcast_in_dim.2
  228.4 4.6 %all-to-all-start.2 = ((bf16[32,8,16,128]{3,2,1,0:T(8,128)(2,1)}), bf16[32,8,16,128]{3,2,1,0:T(8,128)(2,1)S(1)}, u32[]{:S(2)}, u32[]{:S(2)}) async-start(bf16[32,8,16,128]{3,2,1,0:T(8,128)(2,1)} %broadcast_in_dim.2), calls=%async_computation.2 | async-start | bytes 2097152 | tf_op jit(solution)/shard_map/all_to_all | solution.py:173
  232.9 1.0 fusion.2
  233.9 0.1 reshape.69
  234.0 0.8 copy.61
  234.8 25.9 %all-to-all-done.2 = bf16[32,8,16,128]{3,2,1,0:T(8,128)(2,1)S(1)} async-done(((bf16[32,8,16,128]{3,2,1,0:T(8,128)(2,1)}), bf16[32,8,16,128]{3,2,1,0:T(8,128)(2,1)S(1)}, u32[]{:S(2)}, u32[]{:S(2)}) %all-to-all-start.2) | async-done | bytes 1048608 | tf_op jit(solution)/shard_map/all_to_all | solution.py:173
  260.7 0.2 copy.47
  260.9 0.1 slice.20
  260.9 0.1 copy_bitcast_fusion
  261.1 1.4 slice.21
  262.5 0.6 copy.62
  (4 shorter events, 0.1 us)
Async XLA Ops:
  7.2 151.8 %all-gather.2.cloned.1.call-start = ((), (), s32[]{:S(2)}) async-start(), calls=%async_computation.3 | async-start | bytes 15058944 | tf_op jit(solution)/shard_map/all_gather | solution.py:144
  10.4 53.4 %collective-permute-start = (bf16[7168,256]{1,0:T(8,128)(2,1)}, bf16[7168,256]{1,0:T(8,128)(2,1)}, u32[]{:S(2)}, u32[]{:S(2)}) collective-permute-start(bf16[7168,256]{1,0:T(8,128)(2,1)} %bitcast.29), channel_id=1, source_target_pairs={{0,32},{32,0},{1,33},{33,1},{2,34},{34,2},{3,35},{35,3},{4,36},{36... | collective-permute-start | bytes 11010056 | tf_op jit(solution)/shard_map/ppermute | solution.py:146
  10.5 53.3 %collective-permute-start.1 = (bf16[7168,256]{1,0:T(8,128)(2,1)}, bf16[7168,256]{1,0:T(8,128)(2,1)}, u32[]{:S(2)}, u32[]{:S(2)}) collective-permute-start(bf16[7168,256]{1,0:T(8,128)(2,1)} %bitcast.36), channel_id=1, source_target_pairs={{0,32},{32,0},{1,33},{33,1},{2,34},{34,2},{3,35},{35,3},{4,36},{36... | collective-permute-start | bytes 11010056 | tf_op jit(solution)/shard_map/ppermute | solution.py:146
  46.1 1.7 copy-start.4
  47.7 143.3 %collective-permute-start.3 = (bf16[256,3584]{1,0:T(8,128)(2,1)}, bf16[256,3584]{1,0:T(8,128)(2,1)}, u32[]{:S(2)}, u32[]{:S(2)}) collective-permute-start(bf16[256,3584]{1,0:T(8,128)(2,1)} %bitcast.19), channel_id=1, source_target_pairs={{0,32},{32,0},{1,33},{33,1},{2,34},{34,2},{3,35},{35,3},{4,36},{36... | collective-permute-start | bytes 5505032 | tf_op jit(solution)/shard_map/ppermute | solution.py:151
  158.9 2.0 copy-start
  161.0 28.5 %copy-start.2 = (bf16[256,4,896]{2,1,0:T(4,128)(2,1)S(1)}, bf16[256,4,896]{2,1,0:T(4,128)(2,1)}, u32[]{:S(2)}) copy-start(bf16[256,4,896]{2,1,0:T(4,128)(2,1)} %get-tuple-element.10) | copy-start | bytes 5505028
  189.3 1.7 copy-start.1
  189.4 1.6 collective-permute-start.2
  191.0 0.7 copy-start.3
  196.3 30.5 %copy-start.5 = (s32[32]{0:T(128)S(1)}, s32[32]{0:T(128)}, u32[]{:S(2)}) copy-start(s32[32]{0:T(128)} %param.9) | copy-start | bytes 388
  228.4 32.3 %all-to-all-start.2 = ((bf16[32,8,16,128]{3,2,1,0:T(8,128)(2,1)}), bf16[32,8,16,128]{3,2,1,0:T(8,128)(2,1)S(1)}, u32[]{:S(2)}, u32[]{:S(2)}) async-start(bf16[32,8,16,128]{3,2,1,0:T(8,128)(2,1)} %broadcast_in_dim.2), calls=%async_computation.2 | async-start | bytes 2097152 | tf_op jit(solution)/shard_map/all_to_all | solution.py:173
Sparse Core Ops, SparseCore 0:
  12.0 146.8 all-gather.1
